TPU v7x, 128 devices: a whole 4x4x4 slice. The times are simulated.
128 devices in a mesh: gx: 8 (over z_lo, x), gy: 16 (over y, z_hi, core).
Axes of the slice: x: 4, y: 4, z: 4 (z_hi: 2, z_lo: 2; z = z_hi * 2 + z_lo), core: 2. Of those that a mesh axis runs over, the one named last changes fastest.
Arguments:
- state: float32 [3, 64, 128, 2048], P(None, None, 'gx', 'gy'), may hold values from -6 to 6
- parent: float32 [3, 64, 48, 544], P(None, None, 'gx', 'gy'), may hold values from -6 to 6
- stiffness: float32 [64], replicated, may hold values from 0.5 to 1.5
- offsets: int32 [4], replicated, may hold values from -1 to 29, as said below
Outputs:
- advanced: float32 [3, 64, 128, 2048], P(None, None, 'gx', 'gy')
Inputs may be any that keep to these rules, and one draw needn't show every extreme that they name: offsets = (ox, oy, sx, sy): ox from 2 to 13, oy equal to 29, sx and sy each -1 or 1 with sy = -sx.
All inputs are finite; a program needn't handle non-finite values.
Results may differ from a plain program's by a relative error of at most 0.00016.
Values sent between devices are 32-bit elements; how exact they have to be, the bound alone decides.
A program may use at most 128 MiB of HBM per device.

v0:
```python
import functools

import jax
import jax.numpy as jnp
from jax import lax
from jax.experimental import pallas as pl
from jax.experimental.pallas import tpu as pltpu
from jax.sharding import PartitionSpec as P

MESH = pl.DeviceIdType.MESH
F32 = jnp.float32
GX, GY = 8, 16
NZ, BX, BY = 64, 16, 128
CHUNKS = 4
ZC = NZ // CHUNKS
TILES = ZC // 8
PROWS, PCOLS = 6, 34
SLOTS = ((0.375, 0.625, 0.0), (0.125, 0.875, 0.0), (0.0, 0.875, 0.125), (0.0, 0.625, 0.375))


def roll(x, shift):
    shift = shift % 128
    return x if shift == 0 else pltpu.roll(x, shift, 1)


def iota(shape, dim):
    return lax.broadcasted_iota(jnp.int32, shape, dim)


def split_dot(a, b):
    high = a.astype(jnp.bfloat16)
    low = (a - high.astype(F32)).astype(jnp.bfloat16)
    both = jnp.dot(jnp.concatenate([high, low], axis=0), b, preferred_element_type=F32)
    return both[: a.shape[0]] + both[a.shape[0] :]


def bilinear(cell, lower, frac):
    return jnp.where(cell == lower, 1.0 - frac, 0.0) + jnp.where(cell == lower + 1, frac, 0.0)


def kernel(
    s,
    off_hbm,
    stiff_hbm,
    st_hbm,
    par_hbm,
    out_hbm,
    st,
    pin,
    sp,
    own,
    hx,
    yp,
    lp,
    cp,
    cr,
    qm,
    qe,
    pb,
    ub,
    vb,
    ok,
    lr,
    bm,
    be,
    wv,
    sd,
    sx,
    outv,
    tb,
    rsp,
    rsr,
    rsum,
    rnb,
    wr,
    fr,
    hfr,
    csm,
    csr,
    wc,
    off_ref,
    stiff_ref,
    in_sem,
    par_sem,
    smem_sem,
    out_sem,
    send_sem,
    recv_sem,
):
    gx, gy = lax.axis_index("gx"), lax.axis_index("gy")
    here = lambda dx, dy: {"gx": gx + dx, "gy": gy + dy}
    inside = lambda dx, dy: (gx + dx >= 0) & (gx + dx < GX) & (gy + dy >= 0) & (gy + dy < GY)
    ex = GX - 1 if s > 0 else 0
    ey = 0 if s > 0 else GY - 1
    at_x, at_y = gx == ex, gy == ey
    last = 13 if s > 0 else 14

    def lo(d):
        return (2 * d) // 3

    def feeds(src, dst):
        return (src >= lo(dst)) & (src <= lo(dst) + 3) & (dst >= 0) & (dst < GX) & (src >= 0) & (src < GX)

    partners = [(dx, dy, inside(dx, dy)) for dx, dy in ((-1, 0), (1, 0), (0, -1), (0, 1), (-1, 1), (1, -1))]
    partners.append((2 * s, 0, gx == ex - 2 * s))
    partners.append((-2 * s, 0, at_x))
    for d in (-3, -2, 2, 3):
        partners.append((d, 0, at_y & (feeds(gx, gx + d) | feeds(gx + d, gx))))
    barrier = pltpu.get_barrier_semaphore()
    for dx, dy, cond in partners:

        @pl.when(cond)
        def _():
            pl.semaphore_signal(barrier, inc=1, device_id=here(dx, dy), device_id_type=MESH)

    def remote(slot, src, dst, device, recv_slot=None):
        return pltpu.make_async_remote_copy(
            src_ref=src,
            dst_ref=dst,
            send_sem=send_sem.at[slot],
            recv_sem=recv_sem.at[slot if recv_slot is None else recv_slot],
            device_id=device,
            device_id_type=MESH,
        )

    def start(messages):
        for cond, *copy in messages:

            @pl.when(cond)
            def _():
                remote(*copy).start()

    def sent(messages):
        for cond, *copy in messages:

            @pl.when(cond)
            def _():
                remote(*copy).wait_send()

    def arrive(cond, slot, ref, device):
        @pl.when(cond)
        def _():
            remote(slot, ref, ref, device).wait_recv()

    CS_RECV, CS_SEND, RS, NB, FIRST = 0, 4, 10, 12, 14
    ROUND = FIRST + 5 * CHUNKS
    counts = (6, 5, 4)

    def column_messages():
        return [
            (
                at_y & feeds(gx, gx + d),
                CS_SEND + k,
                csm,
                csr.at[gx - lo(gx + d)],
                here(d, 0),
                CS_RECV + gx - lo(gx + d),
            )
            for k, d in enumerate((-3, -2, -1, 1, 2, 3))
        ]

    def row_messages():
        return [(gx == ex - far * s, RS + k, rsp, rsr.at[k], here(far * s, 0)) for k, far in enumerate((2, 1))]

    def strip_messages():
        return [
            (at_x & (gy >= 1) & (gy - 1 <= last), NB, rsum, rnb, here(0, -1)),
            (at_x & (gy + 1 > last) & (gy + 1 < GY), NB + 1, rsum, rnb, here(0, 1)),
        ]

    def first_rows(f):
        return pl.ds(0 if s > 0 else BX - counts[f], counts[f])

    def first_x(c):
        return [
            (
                inside(-s, 0),
                FIRST + 5 * c + f,
                own.at[c, f, first_rows(f)],
                hx.at[c, f, pl.ds(0, counts[f])],
                here(-s, 0),
            )
            for f in range(3)
        ]

    def first_y(c):
        return [
            (inside(0, s), FIRST + 5 * c + 3, yp.at[c], lp.at[c], here(0, s)),
            (inside(-s, s), FIRST + 5 * c + 4, cp.at[c], cr.at[c], here(-s, s)),
        ]

    def p_rows(r, c, first):
        return pb.at[r, c, pl.ds(first + 4, 2)]

    near, far_side = (0, BX) if s > 0 else (BX - 2, -2)

    def near_messages(c):
        return [(inside(-s, 0), round_slot(1, c), p_rows(1, c, near), p_rows(1, c, far_side), here(-s, 0))]

    def round_slot(r, c):
        return ROUND + ((r - 1) * CHUNKS + c) * 4

    def round_messages(r, c):
        k = round_slot(r, c)
        return [
            (inside(-1, 0), k, p_rows(r, c, 0), p_rows(r, c, BX), here(-1, 0)),
            (inside(1, 0), k + 1, p_rows(r, c, BX - 2), p_rows(r, c, -2), here(1, 0)),
            (inside(0, -1), k + 2, ok.at[r, c], lr.at[r, c, 1], here(0, -1)),
            (inside(0, 1), k + 3, ok.at[r, c], lr.at[r, c, 0], here(0, 1)),
        ]

    def receive(r, c):
        k = round_slot(r, c)
        arrive(inside(1, 0), k, p_rows(r, c, BX), here(1, 0))
        arrive(inside(-1, 0), k + 1, p_rows(r, c, -2), here(-1, 0))
        arrive(inside(0, 1), k + 2, lr.at[r, c, 1], here(0, 1))
        arrive(inside(0, -1), k + 3, lr.at[r, c, 0], here(0, -1))

    def chunk_rows(f, c):
        return pl.ds(f * NZ * BX + c * ZC * BX, ZC * BX)

    def load(c, f):
        return pltpu.make_async_copy(st_hbm.at[chunk_rows(f, c)], st.at[chunk_rows(f, c)], in_sem.at[c, f])

    def store(c, f):
        return pltpu.make_async_copy(outv.at[chunk_rows(f, c)], out_hbm.at[chunk_rows(f, c)], out_sem.at[c, f])

    def state_row(c, f, x):
        return st[pl.ds(f * NZ * BX + c * ZC * BX + x, ZC, stride=BX), :]

    for c in range(CHUNKS):
        for f in range(3):
            load(c, f).start()
    par_copy = pltpu.make_async_copy(par_hbm, pin, par_sem)
    par_copy.start()
    scalars = [
        pltpu.make_async_copy(off_hbm, off_ref, smem_sem.at[0]),
        pltpu.make_async_copy(stiff_hbm, stiff_ref, smem_sem.at[1]),
    ]
    for copy in scalars:
        copy.start()

    lane = iota((8, 128), 1)
    group, e = lane >> 3, lane & 7
    lane_c = iota((ZC, 128), 1)
    group_c, e_c = lane_c >> 3, lane_c & 7

    sent_rows = [range(n) if s > 0 else range(BX - n, BX) for n in counts]
    for c in range(CHUNKS):
        for f in range(3):
            load(c, f).wait()
            for x in sent_rows[f]:
                own[c, f, x] = state_row(c, f, x)
    pl.semaphore_wait(barrier, sum(cond.astype(jnp.int32) for _, _, cond in partners))
    for c in range(CHUNKS):
        start(first_x(c))

    def pack(c, carry):
        for f in range(3):
            packed = jnp.zeros((ZC, 128), F32)
            for x in range(BX):
                if x in sent_rows[f]:
                    row = own[c, f, x]
                else:
                    row = state_row(c, f, x)
                    own[c, f, x] = row
                packed = jnp.where(group_c == x, roll(row, 8 * x + (8 if s > 0 else 0)), packed)
            yp[c, f] = packed
            for q in range(TILES // 2):
                one, two = packed[16 * q : 16 * q + 8], packed[16 * q + 8 : 16 * q + 16]
                turn = 0 if s > 0 else 48
                cp[c, f, q] = jnp.where(lane < 64, roll(one, turn), roll(two, turn + 64))
        start(first_y(c))
        return carry

    lax.fori_loop(0, CHUNKS, pack, 0)

    par_copy.wait()
    for copy in scalars:
        copy.wait()
    use_rows = (gx >= 5) if s > 0 else (gx <= 2)
    ox = off_ref[0]

    @pl.when(use_rows)
    def _():
        low = ox + 31 if s > 0 else ox - 2
        for k in range(3):
            tb[k] = jnp.zeros((128, 128), F32)
            weight = [jnp.where(PROWS * gx + row == low + k, 1.0, 0.0) for row in range(PROWS)]
            for f in range(3):
                tb[k, PCOLS * f : PCOLS * f + PCOLS, 0:NZ] = sum(
                    weight[row] * pin[PROWS * f + row] for row in range(PROWS)
                )
        for k in range(3):
            rsp[k] = jnp.transpose(tb[k])[0:NZ]

    start(row_messages())

    @pl.when(at_y)
    def _():
        first_col = 27 if s > 0 else 30
        tb[3] = jnp.zeros((128, 128), F32)
        for row in range(PROWS):
            for f in range(3):
                at = 9 * row + 3 * f
                tb[3, at : at + 3, 0:NZ] = pin[PROWS * f + row, first_col : first_col + 3]
        turned = jnp.transpose(tb[3])
        csm[...] = turned[0:32] + roll(turned[32:64], 64)

    start(column_messages())

    sub = iota((8, 128), 0)
    for t in range(NZ // 8):
        value = jnp.zeros((8, 128), F32)
        for q in range(8):
            value = jnp.where(sub == q, stiff_ref[8 * t + q], value)
        sp[pl.ds(8 * t, 8), :] = 0.5 * value

    def ends(c, carry):
        for r in range(1, 4):

            @pl.when(gx == 0)
            def _():
                pb[r, c, 2:4] = jnp.zeros((2, ZC, 128), F32)

            @pl.when(gx == GX - 1)
            def _():
                pb[r, c, 20:22] = jnp.zeros((2, ZC, 128), F32)

            @pl.when(gy == 0)
            def _():
                lr[r, c, 0] = jnp.zeros((ZC, 128), F32)

            @pl.when(gy == GY - 1)
            def _():
                lr[r, c, 1] = jnp.zeros((ZC, 128), F32)

        return carry

    lax.fori_loop(0, CHUNKS, ends, 0)

    kk = iota((128, 128), 0)
    nn = iota((128, 128), 1)

    @pl.when(at_y)
    def _():
        krow = (kk * 57) >> 9
        krem = kk - 9 * krow
        kf = (krem >= 3).astype(jnp.int32) + (krem >= 6).astype(jnp.int32)
        ks = krem - 3 * kf
        ne = nn & 7
        col = (ne - 4) if s > 0 else ne
        wy = bilinear(ks, (2 * col + 5) >> 3, ((2 * col + 5) & 7).astype(F32) * 0.125)
        wy = jnp.where((col >= 0) & (col < 4) & (kk < 54), wy, 0.0)
        g = nn >> 3
        rows = (g, jnp.where(g < 2, g - 2, jnp.where(g < 4, g + 14, jnp.where(g < 6, g - 8 if s > 0 else g + 14, 0))))
        for k in range(4):
            for m in range(2):
                i = rows[m]
                lower = ox + s + 4 * gx + ((2 * i - 3) >> 3)
                wx = bilinear(PROWS * (lo(gx) + k) + krow, lower, ((2 * i - 3) & 7).astype(F32) * 0.125)
                for f in range(3):
                    wc[f, m, 128 * k : 128 * k + 128] = jnp.where(kf == f, wx * wy, 0.0).astype(jnp.bfloat16)

        for k in range(4):
            src = lo(gx) + k

            @pl.when(src == gx)
            def _():
                csr[k] = csm[...]

            @pl.when(src != gx)
            def _():
                remote(CS_RECV + k, csm, csr.at[k], here(src - gx, 0)).wait_recv()

        parts = [jnp.concatenate([csr[k], roll(csr[k], 64)], axis=0) for k in range(4)]
        column = jnp.concatenate(parts, axis=1)
        for f in range(3):
            for m, dest in enumerate((qm, qe)):
                total = split_dot(column, wc[f, m])
                for c in range(CHUNKS):
                    dest[c, f] = total[c * ZC : (c + 1) * ZC]

    @pl.when(at_x)
    def _():
        for k, far in enumerate((2, 1)):
            remote(RS + k, rsp, rsr.at[k], here(-far * s, 0)).wait_recv()
        for k in range(3):
            rsum[k] = rsp[k] + rsr[0, k] + rsr[1, k]

    start(strip_messages())

    @pl.when(at_x)
    def _():
        base = 28 if s > 0 else 30
        other = jnp.where(gy <= last, gy + 1, gy - 1)

        def weights(block, f, j):
            lower = base + 32 * gy + ((2 * j - 3) >> 3)
            frac = ((2 * j - 3) & 7).astype(F32) * 0.125
            valid = (kk >= PCOLS * f) & (kk < PCOLS * f + PCOLS)
            return jnp.where(valid, bilinear(PCOLS * block + kk - PCOLS * f, lower, frac), 0.0)

        ne = nn & 7
        for b, block in enumerate((gy, other)):
            kr = slice(128 * b, 128 * b + 128)
            for f in range(3):
                wr[f, kr] = weights(block, f, nn).astype(jnp.bfloat16)
                wr[3 + f, kr] = weights(block, f, ne - 4).astype(jnp.bfloat16)
                wr[6 + f, kr] = weights(block, f, ne + 124).astype(jnp.bfloat16)

    edge = lane_c < 4 if s > 0 else lane_c >= 124
    strip = 12 if s > 0 else 0
    ends_x = ((gx == 0) & (lane_c < 16)) | ((gx == GX - 1) & (lane_c >= 16) & (lane_c < 32))
    ends_l, ends_r = (gy == 0) & (e_c < 4), (gy == GY - 1) & (e_c >= 4)
    ends_y = ((gy == 0) & ((e_c < 2) | (e_c == 4))) | ((gy == GY - 1) & ((e_c == 2) | (e_c == 3) | (e_c == 5)))
    spans = ((pb, 4, -4, 22), (ub, 3, -3, 20), (vb, 2, -2, 18)) if s > 0 else ((pb, 4, -2, 22), (ub, 3, -1, 20), (vb, 2, 0, 18))

    def held(i):
        return 0 <= i + 4 * s < BX

    def source(c, f, i):
        old = i + 4 * s
        if held(i):
            return own[c, f, old]
        return hx[c, f, old - BX if s > 0 else old + counts[f]]

    def extra_group(i):
        return {-4: 4, -3: 5, -2: 0, -1: 1, 16: 2, 17: 3, 18: 4, 19: 5}[i]

    def assemble(c, mine):
        for f, (dest, base, first, count) in enumerate(spans):
            main, extra = qm[c, f], qe[c, f]
            for i in range(first, first + count):
                if held(i) != mine:
                    continue
                if 0 <= i < BX:
                    side = roll(main, -(8 * i + 4))
                else:
                    side = roll(extra, -(8 * extra_group(i) + 4))
                dest[0, c, i + base] = jnp.where(edge, side, roll(source(c, f, i), 4 * s))

    def late_columns(c):
        for f, last_row in enumerate(((18, -2), (17, -1), (16, 0))):
            main, extra = bm[c, f], be[c, f]
            for i in range(12, last_row[0]) if s > 0 else range(last_row[1], 4):
                row = source(c, f, i)
                if 0 <= i < BX:
                    main = jnp.where(group_c == i, roll(row, 8 * i + (8 if s > 0 else 0)), main)
                else:
                    g = extra_group(i)
                    extra = jnp.where(group_c == g, roll(row, 8 * g + (8 if s > 0 else 0)), extra)
            bm[c, f] = main
            be[c, f] = extra

    def windows(c):
        q = [(qm[c, f], jnp.where(ends_x, 0.0, qe[c, f])) for f in range(3)]
        b = [(bm[c, f], jnp.where(ends_x, 0.0, be[c, f])) for f in range(3)]
        return (q, b) if s > 0 else (b, q)

    def new_v(p, v, ends):
        return jnp.where(ends, 0.0, v - 0.5 * (roll(p, -1) - roll(p, 1)))

    def put_sides(dest, c, pl_, pr_, vl_, vr_):
        dest[c] = jnp.where(
            e_c == 0, roll(pr_, -4), jnp.where(e_c == 1, roll(pl_, -2), jnp.where(e_c == 2, roll(vr_, -2), vl_))
        )

    def up(main, extra):
        return jnp.where(lane_c < 8, roll(extra, -8), roll(main, 8))

    def down(main, extra):
        return jnp.where(lane_c >= 120, roll(extra, 104), roll(main, -8))

    def window_step(fields, ends, speed):
        (p, px), (u, ux), (v, _) = fields
        u1 = u - 0.5 * (down(p, px) - up(p, px))
        slope = jnp.where(lane_c < 16, roll(p, 8) - roll(px, 8), roll(px, -8) - roll(p, 24))
        u1x = jnp.where(ends_x, 0.0, ux - 0.5 * slope)
        v1 = new_v(p, v, ends)
        p1 = p - speed * ((down(u1, u1x) - up(u1, u1x)) + (roll(v1, -1) - roll(v1, 1)))
        return jnp.where(ends, 0.0, p1), v1

    def step(r, c, first, count):
        final = isinstance(r, int) and r == 3
        packs = not final and not (isinstance(r, int) and r == 0)

        def tile(t):
            zr = pl.ds(8 * t, 8)
            side, extra = sd[c, zr], sx[c, zr]
            speed = sp[pl.ds(pl.multiple_of(c * ZC + 8 * t, 8), 8), :]
            p = {n: pb[r, c, n + 4, zr] for n in range(first - 2, first + count + 2)}
            u = {}
            for n in range(first - 1, first + count + 1):
                new = ub[r, c, n + 3, zr] - 0.5 * (p[n + 1] - p[n - 1])
                if n == -1:
                    new = jnp.where(gx == 0, 0.0, new)
                if n == BX:
                    new = jnp.where(gx == GX - 1, 0.0, new)
                u[n] = new
                mine = first <= n < first + count or (n == -1 and first == 0) or (n == BX and first + count == BX)
                if not final and mine and -1 <= n <= BX:
                    ub[r + 1, c, n + 3, zr] = new
            pack = jnp.zeros((8, 128), F32)
            for x in range(first, first + count):
                near_side, g = (side, x) if 0 <= x < BX else (extra, extra_group(x))
                side_p = roll(near_side, -(8 * g + 1))
                before = jnp.where(lane == 0, side_p, roll(p[x], 1))
                after = jnp.where(lane == 127, side_p, roll(p[x], -1))
                v = vb[r, c, x + 2, zr] - 0.5 * (after - before)
                side_v = roll(near_side, -(8 * g + 3))
                before = jnp.where(lane == 0, side_v, roll(v, 1))
                after = jnp.where(lane == 127, side_v, roll(v, -1))
                new_p = p[x] - speed * ((u[x + 1] - u[x - 1]) + (after - before))
                if x < 0:
                    new_p = jnp.where(gx == 0, 0.0, new_p)
                if x >= BX:
                    new_p = jnp.where(gx == GX - 1, 0.0, new_p)
                if final:
                    for f, value in enumerate((new_p, u[x], v)):
                        outv[pl.ds(f * NZ * BX + (c * ZC + 8 * t) * BX + x, 8, stride=BX), :] = value
                else:
                    pb[r + 1, c, x + 4, zr] = new_p
                    if 0 <= x < BX:
                        vb[r + 1, c, x + 2, zr] = v
                    if packs:
                        pack = jnp.where(group == x, roll(new_p, 8 * x + 2), pack)
            if packs:
                ok[r + 1, c, zr] = pack

        for t in range(TILES):
            tile(t)

    early, late = ((-2, 12), (10, 6)) if s > 0 else ((6, 12), (0, 6))

    def begin(c, carry):
        arrive(inside(0, -s), FIRST + 5 * c + 3, lp.at[c], here(0, -s))
        arrive(inside(s, -s), FIRST + 5 * c + 4, cr.at[c], here(s, -s))

        @pl.when(jnp.logical_not(at_y))
        def _():
            for f in range(3):
                for t in range(TILES):
                    zr, w = pl.ds(8 * t, 8), t % 2
                    corner, side = cr[c, f, t // 2], lp[c, f, zr]
                    if s > 0:
                        qm[c, f, zr] = jnp.where(lane < 96, roll(side, -32), roll(corner, 96 - 64 * w))
                        qe[c, f, zr] = jnp.where(
                            lane < 16, roll(side, -16), jnp.where(lane < 32, roll(corner, -16 - 64 * w), roll(side, 32))
                        )
                    else:
                        qm[c, f, zr] = jnp.where(lane < 32, roll(corner, -16 - 64 * w), roll(side, 32))
                        qe[c, f, zr] = jnp.where(lane < 16, roll(corner, -64 * w), roll(side, -80))

        for f in range(3):
            mine = yp[c, f]
            bm[c, f] = roll(mine, -32 * s)
            be[c, f] = roll(mine, -16 if s > 0 else -80)
        assemble(c, True)

        @pl.when(gx == GX - 1 - ex)
        def _():
            pb[0, c, pl.ds(0 if s > 0 else 20, 4)] = jnp.zeros((4, ZC, 128), F32)

        lw, rw = windows(c)
        for dest, k in ((sd, 0), (sx, 1)):
            (pl_, vl_), (pr_, vr_) = [(w[0][k], w[2][k]) for w in (lw, rw)]
            pl_, pr_ = jnp.where(ends_l, 0.0, pl_), jnp.where(ends_r, 0.0, pr_)
            put_sides(dest, c, pl_, pr_, new_v(pl_, vl_, ends_l), new_v(pr_, vr_, ends_r))
        step(0, c, *early)
        start(near_messages(c))
        return carry

    lax.fori_loop(0, CHUNKS, begin, 0)

    @pl.when(at_x)
    def _():
        @pl.when(gy <= last)
        def _():
            remote(NB, rsum, rnb, here(0, 1)).wait_recv()

        @pl.when(gy > last)
        def _():
            remote(NB + 1, rsum, rnb, here(0, -1)).wait_recv()

        group_z = iota((NZ, 128), 1) >> 3
        rows = jnp.concatenate([jnp.concatenate([rsum[k], rnb[k]], axis=1) for k in range(3)], axis=0)
        for n in range(9):
            total = split_dot(rows, wr[n])
            slots = [total[NZ * k : NZ * k + NZ] for k in range(3)]
            strips = [sum(w * x for w, x in zip(SLOTS[r], slots) if w) for r in range(4)]
            if n < 3:
                for r in range(4):
                    for c in range(CHUNKS):
                        fr[c, n, r] = strips[r][c * ZC : (c + 1) * ZC]
            else:
                total = jnp.zeros((NZ, 128), F32)
                for r in range(4):
                    total = jnp.where(group_z == strip + r, strips[r], total)
                for c in range(CHUNKS):
                    hfr[c, n - 3] = total[c * ZC : (c + 1) * ZC]

    def complete(c, carry):
        for f in range(3):
            arrive(inside(s, 0), FIRST + 5 * c + f, hx.at[c, f, pl.ds(0, counts[f])], here(s, 0))
        assemble(c, False)
        late_columns(c)

        @pl.when(at_x)
        def _():
            for r in range(4):
                for f, (dest, base, _, _) in enumerate(spans):
                    dest[0, c, base + strip + r] = fr[c, f, r]
            pb[0, c, pl.ds(20 if s > 0 else 2, 2)] = jnp.zeros((2, ZC, 128), F32)
            strip_rows = (group_c >= strip) & (group_c < strip + 4)
            for f in range(3):
                for dest, region in ((qm, 0 if s > 0 else 1), (bm, 1 if s > 0 else 0)):
                    dest[c, f] = jnp.where(strip_rows, hfr[c, 3 * region + f], dest[c, f])

        lw, rw = windows(c)
        speed = window_speed(c)
        lw = [(jnp.where(ends_l, 0.0, m), jnp.where(ends_l, 0.0, x)) for m, x in lw]
        rw = [(jnp.where(ends_r, 0.0, m), jnp.where(ends_r, 0.0, x)) for m, x in rw]
        pl1, vl1 = window_step(lw, ends_l, speed)
        pr1, vr1 = window_step(rw, ends_r, speed)
        put_sides(sd, c, lw[0][0], rw[0][0], vl1, vr1)
        step(0, c, *late)
        arrive(inside(s, 0), round_slot(1, c), p_rows(1, c, far_side), here(s, 0))
        vl2, vr2 = new_v(pl1, vl1, ends_l), new_v(pr1, vr1, ends_r)
        put_sides(sd, c, pl1, pr1, vl2, vr2)
        wv[c] = jnp.where(e_c < 5, roll(vl2, 1), roll(vr2, 1))
        step(1, c, 0, BX)
        start(round_messages(2, c))
        return carry

    def window_speed(c):
        return sp[pl.ds(pl.multiple_of(c * ZC, ZC), ZC), :]

    lax.fori_loop(0, CHUNKS, complete, 0)

    def gather(r, c):
        receive(r, c)
        mine = ok[r, c]
        halo = jnp.where(e_c < 2, lr[r, c, 0], jnp.where(e_c < 4, lr[r, c, 1], wv[c]))
        halo = jnp.where(ends_y, 0.0, halo)
        slope = jnp.where(e_c == 4, roll(mine, 2) - roll(halo, 4), roll(halo, 2) - roll(mine, 4))
        wind = jnp.where(ends_y, 0.0, halo - 0.5 * slope)
        wv[c] = wind
        sd[c] = jnp.where(
            e_c == 0,
            roll(halo, -2),
            jnp.where(e_c == 1, halo, jnp.where(e_c == 2, roll(wind, -3), roll(wind, -1))),
        )

    def middle(c, carry):
        gather(2, c)
        step(2, c, 0, BX)
        start(round_messages(3, c))
        return carry

    lax.fori_loop(0, CHUNKS, middle, 0)

    def finish(c, carry):
        gather(3, c)
        step(3, c, 0, BX)
        for f in range(3):
            store(c, f).start()
        return carry

    lax.fori_loop(0, CHUNKS, finish, 0)

    sent(column_messages())
    sent(row_messages())
    sent(strip_messages())

    def settle(c, carry):
        sent(first_x(c))
        sent(first_y(c))
        sent(near_messages(c))
        for r in range(2, 4):
            sent(round_messages(r, c))
        for f in range(3):
            store(c, f).wait()
        return carry

    lax.fori_loop(0, CHUNKS, settle, 0)


def move(s, state, parent, stiffness, offsets):
    vmem = lambda *shape: pltpu.VMEM(shape, F32)
    sems = 14 + CHUNKS * 5 + 3 * CHUNKS * 4
    scratch = [
        vmem(3 * NZ * BX, 128),
        vmem(3 * PROWS, PCOLS, NZ),
        vmem(NZ, 128),
        vmem(CHUNKS, 3, BX, ZC, 128),
        vmem(CHUNKS, 3, 6, ZC, 128),
        vmem(CHUNKS, 3, ZC, 128),
        vmem(CHUNKS, 3, ZC, 128),
        vmem(CHUNKS, 3, TILES // 2, 8, 128),
        vmem(CHUNKS, 3, TILES // 2, 8, 128),
        vmem(CHUNKS, 3, ZC, 128),
        vmem(CHUNKS, 3, ZC, 128),
        vmem(4, CHUNKS, 24, ZC, 128),
        vmem(4, CHUNKS, 22, ZC, 128),
        vmem(4, CHUNKS, 20, ZC, 128),
        vmem(4, CHUNKS, ZC, 128),
        vmem(4, CHUNKS, 2, ZC, 128),
        vmem(CHUNKS, 3, ZC, 128),
        vmem(CHUNKS, 3, ZC, 128),
        vmem(CHUNKS, ZC, 128),
        vmem(CHUNKS, ZC, 128),
        vmem(CHUNKS, ZC, 128),
        vmem(3 * NZ * BX, 128),
        vmem(4, 128, 128),
        vmem(3, NZ, 128),
        vmem(2, 3, NZ, 128),
        vmem(3, NZ, 128),
        vmem(3, NZ, 128),
        pltpu.VMEM((9, 256, 128), jnp.bfloat16),
        vmem(CHUNKS, 3, 4, ZC, 128),
        vmem(CHUNKS, 6, ZC, 128),
        vmem(32, 128),
        vmem(4, 32, 128),
        pltpu.VMEM((3, 2, 512, 128), jnp.bfloat16),
        pltpu.SMEM((4,), jnp.int32),
        pltpu.SMEM((NZ,), F32),
        pltpu.SemaphoreType.DMA((CHUNKS, 3)),
        pltpu.SemaphoreType.DMA,
        pltpu.SemaphoreType.DMA((2,)),
        pltpu.SemaphoreType.DMA((CHUNKS, 3)),
        pltpu.SemaphoreType.DMA((sems,)),
        pltpu.SemaphoreType.DMA((sems,)),
    ]
    hbm = pl.BlockSpec(memory_space=pltpu.HBM)
    return pl.pallas_call(
        functools.partial(kernel, s),
        out_shape=jax.ShapeDtypeStruct((3 * NZ * BX, BY), F32),
        in_specs=[hbm, hbm, hbm, hbm],
        out_specs=hbm,
        scratch_shapes=scratch,
        compiler_params=pltpu.CompilerParams(
            collective_id=0 if s > 0 else 1, has_side_effects=True, vmem_limit_bytes=48 * 2**20
        ),
    )(offsets, stiffness, state, parent)


def per_device(state, parent, stiffness, offsets):
    flat = state.reshape(3 * NZ * BX, BY)
    cells = parent.transpose(0, 2, 3, 1).reshape(3 * PROWS, PCOLS, NZ)
    out = lax.cond(
        offsets[2] > 0, functools.partial(move, 1), functools.partial(move, -1), flat, cells, stiffness, offsets
    )
    return out.reshape(3, NZ, BX, BY)


def solution(mesh):
    return jax.shard_map(
        per_device,
        mesh=mesh,
        in_specs=(P(None, None, "gx", "gy"), P(None, None, "gx", "gy"), P(), P()),
        out_specs=P(None, None, "gx", "gy"),
        check_vma=False,
    )
```

profile of v0, /device:TPU:6, one launch (start us, length us, event | category | flops | bytes accessed | tf_op | source)
XLA Modules:
  0.0 41.6 jit_solution(6325360936938266797)
XLA Ops:
  0.0 1.2 %slice.3 = s32[1]{0:T(128)} slice(s32[4]{0:T(128)} %param.9), slice={[2:3]} | slice | bytes 8 | tf_op jit(solution)/shard_map/slice | solution.py:752
  1.9 38.5 %conditional.1 = (f32[3,64,16,128]{3,2,1,0:T(8,128)S(1)}) conditional(s32[]{:T(128)} %bitcast.6, (s32[4]{0:T(128)}, f32[64]{0:T(128)}, f32[3,64,16,128]{3,2,1,0:T(8,128)}, f32[3,6,34,64]{3,2,1,0:T(8,128)}) %tuple.18, (s32[4]{0:T(128)}, f32[64]{0:T(128)}, f32[3,64,16,128]{3,2,1,0:T(8,128)}, f32[3,6,34,64]{3,2,1,0:T(8,128)}) %tuple.19), branch_computations={%region_0.0_spmd, %region_1.0_spmd} | conditional | bytes 8 | solution.py:751
  1.9 38.5 %branch_1_fun.1 = f32[3072,128]{1,0:T(8,128)S(1)} custom-call(s32[4]{0:T(128)} %get-tuple-element.29.off_hbm, f32[64]{0:T(128)} %get-tuple-element.41.stiff_hbm, f32[3072,128]{1,0:T(8,128)} %bitcast.11, f32[18,34,64]{2,1,0:T(8,128)} %bitcast.15), custom_call_target="tpu_custom_call" | custom-call | tf_op jit(solution)/shard_map/cond/branch_1_fun/pallas_call | solution.py:736
  40.4 1.1 %copy.14 = f32[3,64,16,128]{3,2,1,0:T(8,128)} copy(f32[3,64,16,128]{3,2,1,0:T(8,128)S(1)} %get-tuple-element.33) | data formatting | bytes 3145728
where the time goes:
time: 41.7 us; the launch traced here: 41.6 us
  Pallas kernels  38.5 us (92%)
  local copies, waits for them, and re-layouts  2.38 us (6%)
  between operations  0.66 us (2%)
    pallas_call x1, Pallas kernels, move(): pl.pallas_call(functools.partial(kernel, s), out_shape=jax.ShapeDtypeStru...  38.5 us
    slice x1, local copies, waits for them, and re-layouts, per_device(): offsets[2] > 0  1.24 us
    unnamed x1, local copies, waits for them, and re-layouts  1.15 us

commit v1 on v0

--- a/solution.py
+++ b/solution.py
@@ -12,6 +12,7 @@
 GX, GY = 8, 16
 NZ, BX, BY = 64, 16, 128
 CHUNKS = 4
+AHEAD = 2
 ZC = NZ // CHUNKS
 TILES = ZC // 8
 PROWS, PCOLS = 6, 34
@@ -245,15 +246,36 @@
     lane_c = iota((ZC, 128), 1)
     group_c, e_c = lane_c >> 3, lane_c & 7
 
+    par_copy.wait()
+    for copy in scalars:
+        copy.wait()
+    use_rows = (gx >= 5) if s > 0 else (gx <= 2)
+    ox = off_ref[0]
+
+    @pl.when(use_rows)
+    def _():
+        low = ox + 31 if s > 0 else ox - 2
+        for k in range(3):
+            tb[k] = jnp.zeros((128, 128), F32)
+            weight = [jnp.where(PROWS * gx + row == low + k, 1.0, 0.0) for row in range(PROWS)]
+            for f in range(3):
+                tb[k, PCOLS * f : PCOLS * f + PCOLS, 0:NZ] = sum(
+                    weight[row] * pin[PROWS * f + row] for row in range(PROWS)
+                )
+        for k in range(3):
+            rsp[k] = jnp.transpose(tb[k])[0:NZ]
+
     sent_rows = [range(n) if s > 0 else range(BX - n, BX) for n in counts]
     for c in range(CHUNKS):
         for f in range(3):
             load(c, f).wait()
             for x in sent_rows[f]:
                 own[c, f, x] = state_row(c, f, x)
-    pl.semaphore_wait(barrier, sum(cond.astype(jnp.int32) for _, _, cond in partners))
-    for c in range(CHUNKS):
-        start(first_x(c))
+        if c == 0:
+            pl.semaphore_wait(barrier, sum(cond.astype(jnp.int32) for _, _, cond in partners))
+            start(row_messages())
+        if c < AHEAD:
+            start(first_x(c))
 
     def pack(c, carry):
         for f in range(3):
@@ -274,27 +296,6 @@
         return carry
 
     lax.fori_loop(0, CHUNKS, pack, 0)
-
-    par_copy.wait()
-    for copy in scalars:
-        copy.wait()
-    use_rows = (gx >= 5) if s > 0 else (gx <= 2)
-    ox = off_ref[0]
-
-    @pl.when(use_rows)
-    def _():
-        low = ox + 31 if s > 0 else ox - 2
-        for k in range(3):
-            tb[k] = jnp.zeros((128, 128), F32)
-            weight = [jnp.where(PROWS * gx + row == low + k, 1.0, 0.0) for row in range(PROWS)]
-            for f in range(3):
-                tb[k, PCOLS * f : PCOLS * f + PCOLS, 0:NZ] = sum(
-                    weight[row] * pin[PROWS * f + row] for row in range(PROWS)
-                )
-        for k in range(3):
-            rsp[k] = jnp.transpose(tb[k])[0:NZ]
-
-    start(row_messages())
 
     @pl.when(at_y)
     def _():
@@ -380,34 +381,6 @@
                 total = split_dot(column, wc[f, m])
                 for c in range(CHUNKS):
                     dest[c, f] = total[c * ZC : (c + 1) * ZC]
-
-    @pl.when(at_x)
-    def _():
-        for k, far in enumerate((2, 1)):
-            remote(RS + k, rsp, rsr.at[k], here(-far * s, 0)).wait_recv()
-        for k in range(3):
-            rsum[k] = rsp[k] + rsr[0, k] + rsr[1, k]
-
-    start(strip_messages())
-
-    @pl.when(at_x)
-    def _():
-        base = 28 if s > 0 else 30
-        other = jnp.where(gy <= last, gy + 1, gy - 1)
-
-        def weights(block, f, j):
-            lower = base + 32 * gy + ((2 * j - 3) >> 3)
-            frac = ((2 * j - 3) & 7).astype(F32) * 0.125
-            valid = (kk >= PCOLS * f) & (kk < PCOLS * f + PCOLS)
-            return jnp.where(valid, bilinear(PCOLS * block + kk - PCOLS * f, lower, frac), 0.0)
-
-        ne = nn & 7
-        for b, block in enumerate((gy, other)):
-            kr = slice(128 * b, 128 * b + 128)
-            for f in range(3):
-                wr[f, kr] = weights(block, f, nn).astype(jnp.bfloat16)
-                wr[3 + f, kr] = weights(block, f, ne - 4).astype(jnp.bfloat16)
-                wr[6 + f, kr] = weights(block, f, ne + 124).astype(jnp.bfloat16)
 
     edge = lane_c < 4 if s > 0 else lane_c >= 124
     strip = 12 if s > 0 else 0
@@ -534,6 +507,14 @@
     early, late = ((-2, 12), (10, 6)) if s > 0 else ((6, 12), (0, 6))
 
     def begin(c, carry):
+        @pl.when(at_x & (c == CHUNKS // 2))
+        def _():
+            for k, far in enumerate((2, 1)):
+                remote(RS + k, rsp, rsr.at[k], here(-far * s, 0)).wait_recv()
+            for k in range(3):
+                rsum[k] = rsp[k] + rsr[0, k] + rsr[1, k]
+            start(strip_messages())
+
         arrive(inside(0, -s), FIRST + 5 * c + 3, lp.at[c], here(0, -s))
         arrive(inside(s, -s), FIRST + 5 * c + 4, cr.at[c], here(s, -s))
 
@@ -569,9 +550,33 @@
             put_sides(dest, c, pl_, pr_, new_v(pl_, vl_, ends_l), new_v(pr_, vr_, ends_r))
         step(0, c, *early)
         start(near_messages(c))
+
+        @pl.when(c + AHEAD < CHUNKS)
+        def _():
+            start(first_x(c + AHEAD))
+
         return carry
 
     lax.fori_loop(0, CHUNKS, begin, 0)
+
+    @pl.when(at_x)
+    def _():
+        base = 28 if s > 0 else 30
+        other = jnp.where(gy <= last, gy + 1, gy - 1)
+
+        def weights(block, f, j):
+            lower = base + 32 * gy + ((2 * j - 3) >> 3)
+            frac = ((2 * j - 3) & 7).astype(F32) * 0.125
+            valid = (kk >= PCOLS * f) & (kk < PCOLS * f + PCOLS)
+            return jnp.where(valid, bilinear(PCOLS * block + kk - PCOLS * f, lower, frac), 0.0)
+
+        ne = nn & 7
+        for b, block in enumerate((gy, other)):
+            kr = slice(128 * b, 128 * b + 128)
+            for f in range(3):
+                wr[f, kr] = weights(block, f, nn).astype(jnp.bfloat16)
+                wr[3 + f, kr] = weights(block, f, ne - 4).astype(jnp.bfloat16)
+                wr[6 + f, kr] = weights(block, f, ne + 124).astype(jnp.bfloat16)
 
     @pl.when(at_x)
     def _():

time: 41.7 us -> 40 us (0.959)
  the two profiles are of different devices: /device:TPU:6 before, /device:TPU:49 now
where the time goes in v1:
time: 40 us; the launch traced here: 39.9 us
  Pallas kernels  36.8 us (92%)
  local copies, waits for them, and re-layouts  2.38 us (6%)
  between operations  0.66 us (2%)
    pallas_call x1, Pallas kernels, move(): pl.pallas_call(functools.partial(kernel, s), out_shape=jax.ShapeDtypeStru...  36.8 us
    slice x1, local copies, waits for them, and re-layouts, per_device(): offsets[2] > 0  1.24 us
    unnamed x1, local copies, waits for them, and re-layouts  1.15 us

profile of v1, /device:TPU:49, one launch (start us, length us, event | category | flops | bytes accessed | tf_op | source)
XLA Modules:
  0.0 39.9 jit_solution(9413893696585833108)
XLA Ops:
  0.0 1.2 %slice.3 = s32[1]{0:T(128)} slice(s32[4]{0:T(128)} %param.9), slice={[2:3]} | slice | bytes 8 | tf_op jit(solution)/shard_map/slice | solution.py:757
  1.9 36.8 %conditional.1 = (f32[3,64,16,128]{3,2,1,0:T(8,128)S(1)}) conditional(s32[]{:T(128)} %bitcast.6, (s32[4]{0:T(128)}, f32[64]{0:T(128)}, f32[3,64,16,128]{3,2,1,0:T(8,128)}, f32[3,6,34,64]{3,2,1,0:T(8,128)}) %tuple.18, (s32[4]{0:T(128)}, f32[64]{0:T(128)}, f32[3,64,16,128]{3,2,1,0:T(8,128)}, f32[3,6,34,64]{3,2,1,0:T(8,128)}) %tuple.19), branch_computations={%region_0.0_spmd, %region_1.0_spmd} | conditional | bytes 8 | solution.py:756
  1.9 36.8 %branch_1_fun.1 = f32[3072,128]{1,0:T(8,128)S(1)} custom-call(s32[4]{0:T(128)} %get-tuple-element.29.off_hbm, f32[64]{0:T(128)} %get-tuple-element.41.stiff_hbm, f32[3072,128]{1,0:T(8,128)} %bitcast.11, f32[18,34,64]{2,1,0:T(8,128)} %bitcast.15), custom_call_target="tpu_custom_call" | custom-call | tf_op jit(solution)/shard_map/cond/branch_1_fun/pallas_call | solution.py:741
  38.7 1.1 %copy.14 = f32[3,64,16,128]{3,2,1,0:T(8,128)} copy(f32[3,64,16,128]{3,2,1,0:T(8,128)S(1)} %get-tuple-element.33) | data formatting | bytes 3145728

commit v2 on v1

--- a/solution.py
+++ b/solution.py
@@ -45,7 +45,7 @@
     stiff_hbm,
     st_hbm,
     par_hbm,
-    out_hbm,
+    out_ref,
     st,
     pin,
     sp,
@@ -67,7 +67,6 @@
     wv,
     sd,
     sx,
-    outv,
     tb,
     rsp,
     rsr,
@@ -84,7 +83,6 @@
     in_sem,
     par_sem,
     smem_sem,
-    out_sem,
     send_sem,
     recv_sem,
 ):
@@ -217,22 +215,15 @@
         arrive(inside(0, 1), k + 2, lr.at[r, c, 1], here(0, 1))
         arrive(inside(0, -1), k + 3, lr.at[r, c, 0], here(0, -1))
 
-    def chunk_rows(f, c):
-        return pl.ds(f * NZ * BX + c * ZC * BX, ZC * BX)
-
-    def load(c, f):
-        return pltpu.make_async_copy(st_hbm.at[chunk_rows(f, c)], st.at[chunk_rows(f, c)], in_sem.at[c, f])
-
-    def store(c, f):
-        return pltpu.make_async_copy(outv.at[chunk_rows(f, c)], out_hbm.at[chunk_rows(f, c)], out_sem.at[c, f])
+    def load(c):
+        rows = pl.ds(c * ZC * BX, ZC * BX)
+        return pltpu.make_async_copy(st_hbm.at[:, rows], st.at[:, rows], in_sem.at[c])
 
     def state_row(c, f, x):
-        return st[pl.ds(f * NZ * BX + c * ZC * BX + x, ZC, stride=BX), :]
-
-    for c in range(CHUNKS):
-        for f in range(3):
-            load(c, f).start()
+        return st[f, pl.ds(c * ZC * BX + x, ZC, stride=BX), :]
+
     par_copy = pltpu.make_async_copy(par_hbm, pin, par_sem)
+    load(0).start()
     par_copy.start()
     scalars = [
         pltpu.make_async_copy(off_hbm, off_ref, smem_sem.at[0]),
@@ -240,6 +231,8 @@
     ]
     for copy in scalars:
         copy.start()
+    for c in range(1, CHUNKS):
+        load(c).start()
 
     lane = iota((8, 128), 1)
     group, e = lane >> 3, lane & 7
@@ -267,15 +260,18 @@
 
     sent_rows = [range(n) if s > 0 else range(BX - n, BX) for n in counts]
     for c in range(CHUNKS):
+        load(c).wait()
         for f in range(3):
-            load(c, f).wait()
             for x in sent_rows[f]:
                 own[c, f, x] = state_row(c, f, x)
         if c == 0:
             pl.semaphore_wait(barrier, sum(cond.astype(jnp.int32) for _, _, cond in partners))
-            start(row_messages())
+            if s < 0:
+                start(row_messages())
         if c < AHEAD:
             start(first_x(c))
+        if c == 0 and s > 0:
+            start(row_messages())
 
     def pack(c, carry):
         for f in range(3):
@@ -491,7 +487,7 @@
                     new_p = jnp.where(gx == GX - 1, 0.0, new_p)
                 if final:
                     for f, value in enumerate((new_p, u[x], v)):
-                        outv[pl.ds(f * NZ * BX + (c * ZC + 8 * t) * BX + x, 8, stride=BX), :] = value
+                        out_ref[pl.ds(f * NZ * BX + (c * ZC + 8 * t) * BX + x, 8, stride=BX), :] = value
                 else:
                     pb[r + 1, c, x + 4, zr] = new_p
                     if 0 <= x < BX:
@@ -668,8 +664,6 @@
     def finish(c, carry):
         gather(3, c)
         step(3, c, 0, BX)
-        for f in range(3):
-            store(c, f).start()
         return carry
 
     lax.fori_loop(0, CHUNKS, finish, 0)
@@ -684,8 +678,6 @@
         sent(near_messages(c))
         for r in range(2, 4):
             sent(round_messages(r, c))
-        for f in range(3):
-            store(c, f).wait()
         return carry
 
     lax.fori_loop(0, CHUNKS, settle, 0)
@@ -695,7 +687,7 @@
     vmem = lambda *shape: pltpu.VMEM(shape, F32)
     sems = 14 + CHUNKS * 5 + 3 * CHUNKS * 4
     scratch = [
-        vmem(3 * NZ * BX, 128),
+        vmem(3, NZ * BX, 128),
         vmem(3 * PROWS, PCOLS, NZ),
         vmem(NZ, 128),
         vmem(CHUNKS, 3, BX, ZC, 128),
@@ -716,7 +708,6 @@
         vmem(CHUNKS, ZC, 128),
         vmem(CHUNKS, ZC, 128),
         vmem(CHUNKS, ZC, 128),
-        vmem(3 * NZ * BX, 128),
         vmem(4, 128, 128),
         vmem(3, NZ, 128),
         vmem(2, 3, NZ, 128),
@@ -730,10 +721,9 @@
         pltpu.VMEM((3, 2, 512, 128), jnp.bfloat16),
         pltpu.SMEM((4,), jnp.int32),
         pltpu.SMEM((NZ,), F32),
-        pltpu.SemaphoreType.DMA((CHUNKS, 3)),
+        pltpu.SemaphoreType.DMA((CHUNKS,)),
         pltpu.SemaphoreType.DMA,
         pltpu.SemaphoreType.DMA((2,)),
-        pltpu.SemaphoreType.DMA((CHUNKS, 3)),
         pltpu.SemaphoreType.DMA((sems,)),
         pltpu.SemaphoreType.DMA((sems,)),
     ]
@@ -742,7 +732,7 @@
         functools.partial(kernel, s),
         out_shape=jax.ShapeDtypeStruct((3 * NZ * BX, BY), F32),
         in_specs=[hbm, hbm, hbm, hbm],
-        out_specs=hbm,
+        out_specs=pl.BlockSpec(memory_space=pltpu.VMEM),
         scratch_shapes=scratch,
         compiler_params=pltpu.CompilerParams(
             collective_id=0 if s > 0 else 1, has_side_effects=True, vmem_limit_bytes=48 * 2**20
@@ -751,7 +741,7 @@
 
 
 def per_device(state, parent, stiffness, offsets):
-    flat = state.reshape(3 * NZ * BX, BY)
+    flat = state.reshape(3, NZ * BX, BY)
     cells = parent.transpose(0, 2, 3, 1).reshape(3 * PROWS, PCOLS, NZ)
     out = lax.cond(
         offsets[2] > 0, functools.partial(move, 1), functools.partial(move, -1), flat, cells, stiffness, offsets

time: 40 us -> 38.4 us (0.960)
  Pallas kernels: 36.8 us -> 35.2 us
    pallas_call x1, Pallas kernels: 36.8 us -> 35.2 us  [move(): pl.pallas_call(functools.partial(kernel, s), out_shape=jax.ShapeDtypeStru...]
where the time goes in v2:
time: 38.4 us; the launch traced here: 38.3 us
  Pallas kernels  35.2 us (92%)
  local copies, waits for them, and re-layouts  2.38 us (6%)
  between operations  0.66 us (2%)
    pallas_call x1, Pallas kernels, move(): pl.pallas_call(functools.partial(kernel, s), out_shape=jax.ShapeDtypeStru...  35.2 us
    slice x1, local copies, waits for them, and re-layouts, per_device(): offsets[2] > 0  1.24 us
    unnamed x1, local copies, waits for them, and re-layouts  1.15 us

profile of v2, /device:TPU:49, one launch (start us, length us, event | category | flops | bytes accessed | tf_op | source)
XLA Modules:
  0.0 38.3 jit_solution(13177779838883678592)
XLA Ops:
  0.0 1.2 %slice.3 = s32[1]{0:T(128)} slice(s32[4]{0:T(128)} %param.9), slice={[2:3]} | slice | bytes 8 | tf_op jit(solution)/shard_map/slice | solution.py:747
  1.9 35.3 %conditional.1 = (f32[3,64,16,128]{3,2,1,0:T(8,128)S(1)}) conditional(s32[]{:T(128)} %bitcast.6, (s32[4]{0:T(128)}, f32[64]{0:T(128)}, f32[3,64,16,128]{3,2,1,0:T(8,128)}, f32[3,6,34,64]{3,2,1,0:T(8,128)}) %tuple.18, (s32[4]{0:T(128)}, f32[64]{0:T(128)}, f32[3,64,16,128]{3,2,1,0:T(8,128)}, f32[3,6,34,64]{3,2,1,0:T(8,128)}) %tuple.19), branch_computations={%region_0.0_spmd, %region_1.0_spmd} | conditional | bytes 8 | solution.py:746
  1.9 35.2 %branch_0_fun.1 = f32[3072,128]{1,0:T(8,128)S(1)} custom-call(s32[4]{0:T(128)} %get-tuple-element.25.off_hbm, f32[64]{0:T(128)} %get-tuple-element.40.stiff_hbm, f32[3,1024,128]{2,1,0:T(8,128)} %bitcast.10, f32[18,34,64]{2,1,0:T(8,128)} %bitcast.14), custom_call_target="tpu_custom_call" | custom-call | tf_op jit(solution)/shard_map/cond/branch_0_fun/pallas_call | solution.py:731
  37.1 1.1 %copy.14 = f32[3,64,16,128]{3,2,1,0:T(8,128)} copy(f32[3,64,16,128]{3,2,1,0:T(8,128)S(1)} %get-tuple-element.33) | data formatting | bytes 3145728

commit v3 on v2

--- a/solution.py
+++ b/solution.py
@@ -50,6 +50,7 @@
     pin,
     sp,
     own,
+    hs,
     hx,
     yp,
     lp,
@@ -143,7 +144,7 @@
 
     CS_RECV, CS_SEND, RS, NB, FIRST = 0, 4, 10, 12, 14
     ROUND = FIRST + 5 * CHUNKS
-    counts = (6, 5, 4)
+    counts, starts = (6, 5, 4), (0, 6, 11)
 
     def column_messages():
         return [
@@ -167,20 +168,8 @@
             (at_x & (gy + 1 > last) & (gy + 1 < GY), NB + 1, rsum, rnb, here(0, 1)),
         ]
 
-    def first_rows(f):
-        return pl.ds(0 if s > 0 else BX - counts[f], counts[f])
-
     def first_x(c):
-        return [
-            (
-                inside(-s, 0),
-                FIRST + 5 * c + f,
-                own.at[c, f, first_rows(f)],
-                hx.at[c, f, pl.ds(0, counts[f])],
-                here(-s, 0),
-            )
-            for f in range(3)
-        ]
+        return [(inside(-s, 0), FIRST + 5 * c, hs.at[c], hx.at[c], here(-s, 0))]
 
     def first_y(c):
         return [
@@ -262,8 +251,8 @@
     for c in range(CHUNKS):
         load(c).wait()
         for f in range(3):
-            for x in sent_rows[f]:
-                own[c, f, x] = state_row(c, f, x)
+            for n, x in enumerate(sent_rows[f]):
+                hs[c, starts[f] + n] = state_row(c, f, x)
         if c == 0:
             pl.semaphore_wait(barrier, sum(cond.astype(jnp.int32) for _, _, cond in partners))
             if s < 0:
@@ -277,11 +266,8 @@
         for f in range(3):
             packed = jnp.zeros((ZC, 128), F32)
             for x in range(BX):
-                if x in sent_rows[f]:
-                    row = own[c, f, x]
-                else:
-                    row = state_row(c, f, x)
-                    own[c, f, x] = row
+                row = state_row(c, f, x)
+                own[c, f, x] = row
                 packed = jnp.where(group_c == x, roll(row, 8 * x + (8 if s > 0 else 0)), packed)
             yp[c, f] = packed
             for q in range(TILES // 2):
@@ -392,7 +378,7 @@
         old = i + 4 * s
         if held(i):
             return own[c, f, old]
-        return hx[c, f, old - BX if s > 0 else old + counts[f]]
+        return hx[c, starts[f] + (old - BX if s > 0 else old + counts[f])]
 
     def extra_group(i):
         return {-4: 4, -3: 5, -2: 0, -1: 1, 16: 2, 17: 3, 18: 4, 19: 5}[i]
@@ -547,9 +533,13 @@
         step(0, c, *early)
         start(near_messages(c))
 
-        @pl.when(c + AHEAD < CHUNKS)
-        def _():
-            start(first_x(c + AHEAD))
+        @pl.when(c == 0)
+        def _():
+            start(first_x(2))
+
+        @pl.when(c == 2)
+        def _():
+            start(first_x(3))
 
         return carry
 
@@ -602,8 +592,7 @@
                     hfr[c, n - 3] = total[c * ZC : (c + 1) * ZC]
 
     def complete(c, carry):
-        for f in range(3):
-            arrive(inside(s, 0), FIRST + 5 * c + f, hx.at[c, f, pl.ds(0, counts[f])], here(s, 0))
+        arrive(inside(s, 0), FIRST + 5 * c, hx.at[c], here(s, 0))
         assemble(c, False)
         late_columns(c)
 
@@ -691,7 +680,8 @@
         vmem(3 * PROWS, PCOLS, NZ),
         vmem(NZ, 128),
         vmem(CHUNKS, 3, BX, ZC, 128),
-        vmem(CHUNKS, 3, 6, ZC, 128),
+        vmem(CHUNKS, 15, ZC, 128),
+        vmem(CHUNKS, 15, ZC, 128),
         vmem(CHUNKS, 3, ZC, 128),
         vmem(CHUNKS, 3, ZC, 128),
         vmem(CHUNKS, 3, TILES // 2, 8, 128),

time: 38.4 us -> 38.1 us (level)
  Pallas kernels: 35.2 us -> 34.6 us
    pallas_call x1, Pallas kernels: 35.2 us -> 34.6 us  [move(): pl.pallas_call(functools.partial(kernel, s), out_shape=jax.ShapeDtypeStru...]
where the time goes in v3:
time: 38.1 us; the launch traced here: 37.6 us
  Pallas kernels  34.6 us (91%)
  local copies, waits for them, and re-layouts  2.38 us (6%)
  between operations  0.66 us (2%)
    pallas_call x1, Pallas kernels, move(): pl.pallas_call(functools.partial(kernel, s), out_shape=jax.ShapeDtypeStru...  34.6 us
    slice x1, local copies, waits for them, and re-layouts, per_device(): offsets[2] > 0  1.24 us
    unnamed x1, local copies, waits for them, and re-layouts  1.15 us

profile of v3, /device:TPU:49, one launch (start us, length us, event | category | flops | bytes accessed | tf_op | source)
XLA Modules:
  0.0 37.6 jit_solution(5494789959203108465)
XLA Ops:
  0.0 1.2 %slice.3 = s32[1]{0:T(128)} slice(s32[4]{0:T(128)} %param.9), slice={[2:3]} | slice | bytes 8 | tf_op jit(solution)/shard_map/slice | solution.py:737
  1.9 34.6 %conditional.1 = (f32[3,64,16,128]{3,2,1,0:T(8,128)S(1)}) conditional(s32[]{:T(128)} %bitcast.6, (s32[4]{0:T(128)}, f32[64]{0:T(128)}, f32[3,64,16,128]{3,2,1,0:T(8,128)}, f32[3,6,34,64]{3,2,1,0:T(8,128)}) %tuple.18, (s32[4]{0:T(128)}, f32[64]{0:T(128)}, f32[3,64,16,128]{3,2,1,0:T(8,128)}, f32[3,6,34,64]{3,2,1,0:T(8,128)}) %tuple.19), branch_computations={%region_0.0_spmd, %region_1.0_spmd} | conditional | bytes 8 | solution.py:736
  1.9 34.6 %branch_0_fun.1 = f32[3072,128]{1,0:T(8,128)S(1)} custom-call(s32[4]{0:T(128)} %get-tuple-element.25.off_hbm, f32[64]{0:T(128)} %get-tuple-element.40.stiff_hbm, f32[3,1024,128]{2,1,0:T(8,128)} %bitcast.10, f32[18,34,64]{2,1,0:T(8,128)} %bitcast.14), custom_call_target="tpu_custom_call" | custom-call | tf_op jit(solution)/shard_map/cond/branch_0_fun/pallas_call | solution.py:721
  36.5 1.1 %copy.14 = f32[3,64,16,128]{3,2,1,0:T(8,128)} copy(f32[3,64,16,128]{3,2,1,0:T(8,128)S(1)} %get-tuple-element.33) | data formatting | bytes 3145728

commit v4 on v3

--- a/solution.py
+++ b/solution.py
@@ -263,6 +263,7 @@
             start(row_messages())
 
     def pack(c, carry):
+        packs = []
         for f in range(3):
             packed = jnp.zeros((ZC, 128), F32)
             for x in range(BX):
@@ -270,10 +271,9 @@
                 own[c, f, x] = row
                 packed = jnp.where(group_c == x, roll(row, 8 * x + (8 if s > 0 else 0)), packed)
             yp[c, f] = packed
-            for q in range(TILES // 2):
-                one, two = packed[16 * q : 16 * q + 8], packed[16 * q + 8 : 16 * q + 16]
-                turn = 0 if s > 0 else 48
-                cp[c, f, q] = jnp.where(lane < 64, roll(one, turn), roll(two, turn + 64))
+            packs.append(packed)
+        p, u, v = [roll(value, turn) for value, turn in zip(packs, (0, 48, 88) if s > 0 else (-80, -40, -8))]
+        cp[c] = jnp.where(lane_c < 48, p, jnp.where(lane_c < 88, u, v))
         start(first_y(c))
         return carry
 
@@ -486,6 +486,7 @@
         for t in range(TILES):
             tile(t)
 
+    corner_at = (0, 48, 88) if s > 0 else (0, 40, 72)
     early, late = ((-2, 12), (10, 6)) if s > 0 else ((6, 12), (0, 6))
 
     def begin(c, carry):
@@ -503,17 +504,15 @@
         @pl.when(jnp.logical_not(at_y))
         def _():
             for f in range(3):
-                for t in range(TILES):
-                    zr, w = pl.ds(8 * t, 8), t % 2
-                    corner, side = cr[c, f, t // 2], lp[c, f, zr]
-                    if s > 0:
-                        qm[c, f, zr] = jnp.where(lane < 96, roll(side, -32), roll(corner, 96 - 64 * w))
-                        qe[c, f, zr] = jnp.where(
-                            lane < 16, roll(side, -16), jnp.where(lane < 32, roll(corner, -16 - 64 * w), roll(side, 32))
-                        )
-                    else:
-                        qm[c, f, zr] = jnp.where(lane < 32, roll(corner, -16 - 64 * w), roll(side, 32))
-                        qe[c, f, zr] = jnp.where(lane < 16, roll(corner, -64 * w), roll(side, -80))
+                corner, side, at = cr[c], lp[c, f], corner_at[f]
+                if s > 0:
+                    qm[c, f] = jnp.where(lane_c < 96, roll(side, -32), roll(corner, 96 - at))
+                    qe[c, f] = jnp.where(
+                        lane_c < 16, roll(side, -16), jnp.where(lane_c < 32, roll(corner, -16 - at), roll(side, 32))
+                    )
+                else:
+                    qm[c, f] = jnp.where(lane_c < 32, roll(corner, -16 - at), roll(side, 32))
+                    qe[c, f] = jnp.where(lane_c < 16, roll(corner, -at), roll(side, -80))
 
         for f in range(3):
             mine = yp[c, f]
@@ -620,7 +619,7 @@
         put_sides(sd, c, pl1, pr1, vl2, vr2)
         wv[c] = jnp.where(e_c < 5, roll(vl2, 1), roll(vr2, 1))
         step(1, c, 0, BX)
-        start(round_messages(2, c))
+        start(round_messages(2, c)[2:] + round_messages(2, c)[:2])
         return carry
 
     def window_speed(c):
@@ -645,7 +644,7 @@
     def middle(c, carry):
         gather(2, c)
         step(2, c, 0, BX)
-        start(round_messages(3, c))
+        start(round_messages(3, c)[2:] + round_messages(3, c)[:2])
         return carry
 
     lax.fori_loop(0, CHUNKS, middle, 0)
@@ -684,8 +683,8 @@
         vmem(CHUNKS, 15, ZC, 128),
         vmem(CHUNKS, 3, ZC, 128),
         vmem(CHUNKS, 3, ZC, 128),
-        vmem(CHUNKS, 3, TILES // 2, 8, 128),
-        vmem(CHUNKS, 3, TILES // 2, 8, 128),
+        vmem(CHUNKS, ZC, 128),
+        vmem(CHUNKS, ZC, 128),
         vmem(CHUNKS, 3, ZC, 128),
         vmem(CHUNKS, 3, ZC, 128),
         vmem(4, CHUNKS, 24, ZC, 128),

time: 38.1 us -> 38.6 us (1.013)
  Pallas kernels: 34.6 us -> 35.4 us
    pallas_call x1, Pallas kernels: 34.6 us -> 35.4 us  [move(): pl.pallas_call(functools.partial(kernel, s), out_shape=jax.ShapeDtypeStru...]
where the time goes in v4:
time: 38.6 us; the launch traced here: 38.4 us
  Pallas kernels  35.4 us (92%)
  local copies, waits for them, and re-layouts  2.38 us (6%)
  between operations  0.66 us (2%)
    pallas_call x1, Pallas kernels, move(): pl.pallas_call(functools.partial(kernel, s), out_shape=jax.ShapeDtypeStru...  35.4 us
    slice x1, local copies, waits for them, and re-layouts, per_device(): offsets[2] > 0  1.24 us
    unnamed x1, local copies, waits for them, and re-layouts  1.15 us

profile of v4, /device:TPU:49, one launch (start us, length us, event | category | flops | bytes accessed | tf_op | source)
XLA Modules:
  0.0 38.4 jit_solution(3277349125477773123)
XLA Ops:
  0.0 1.2 %slice.3 = s32[1]{0:T(128)} slice(s32[4]{0:T(128)} %param.9), slice={[2:3]} | slice | bytes 8 | tf_op jit(solution)/shard_map/slice | solution.py:736
  1.9 35.4 %conditional.1 = (f32[3,64,16,128]{3,2,1,0:T(8,128)S(1)}) conditional(s32[]{:T(128)} %bitcast.6, (s32[4]{0:T(128)}, f32[64]{0:T(128)}, f32[3,64,16,128]{3,2,1,0:T(8,128)}, f32[3,6,34,64]{3,2,1,0:T(8,128)}) %tuple.18, (s32[4]{0:T(128)}, f32[64]{0:T(128)}, f32[3,64,16,128]{3,2,1,0:T(8,128)}, f32[3,6,34,64]{3,2,1,0:T(8,128)}) %tuple.19), branch_computations={%region_0.0_spmd, %region_1.0_spmd} | conditional | bytes 8 | solution.py:735
  1.9 35.4 %branch_1_fun.1 = f32[3072,128]{1,0:T(8,128)S(1)} custom-call(s32[4]{0:T(128)} %get-tuple-element.29.off_hbm, f32[64]{0:T(128)} %get-tuple-element.41.stiff_hbm, f32[3,1024,128]{2,1,0:T(8,128)} %bitcast.11, f32[18,34,64]{2,1,0:T(8,128)} %bitcast.15), custom_call_target="tpu_custom_call" | custom-call | tf_op jit(solution)/shard_map/cond/branch_1_fun/pallas_call | solution.py:720
  37.3 1.1 %copy.14 = f32[3,64,16,128]{3,2,1,0:T(8,128)} copy(f32[3,64,16,128]{3,2,1,0:T(8,128)S(1)} %get-tuple-element.33) | data formatting | bytes 3145728

commit v5 on v4

--- a/solution.py
+++ b/solution.py
@@ -456,7 +456,7 @@
                 mine = first <= n < first + count or (n == -1 and first == 0) or (n == BX and first + count == BX)
                 if not final and mine and -1 <= n <= BX:
                     ub[r + 1, c, n + 3, zr] = new
-            pack = jnp.zeros((8, 128), F32)
+            pack = ok[r + 1, c, zr] if packs and first > 0 else jnp.zeros((8, 128), F32)
             for x in range(first, first + count):
                 near_side, g = (side, x) if 0 <= x < BX else (extra, extra_group(x))
                 side_p = roll(near_side, -(8 * g + 1))
@@ -618,8 +618,11 @@
         vl2, vr2 = new_v(pl1, vl1, ends_l), new_v(pr1, vr1, ends_r)
         put_sides(sd, c, pl1, pr1, vl2, vr2)
         wv[c] = jnp.where(e_c < 5, roll(vl2, 1), roll(vr2, 1))
-        step(1, c, 0, BX)
-        start(round_messages(2, c)[2:] + round_messages(2, c)[:2])
+        step(1, c, 0, 2)
+        step(1, c, BX - 2, 2)
+        start(round_messages(2, c)[:2])
+        step(1, c, 2, BX - 4)
+        start(round_messages(2, c)[2:])
         return carry
 
     def window_speed(c):
@@ -643,8 +646,11 @@
 
     def middle(c, carry):
         gather(2, c)
-        step(2, c, 0, BX)
-        start(round_messages(3, c)[2:] + round_messages(3, c)[:2])
+        step(2, c, 0, 2)
+        step(2, c, BX - 2, 2)
+        start(round_messages(3, c)[:2])
+        step(2, c, 2, BX - 4)
+        start(round_messages(3, c)[2:])
         return carry
 
     lax.fori_loop(0, CHUNKS, middle, 0)

time: 38.6 us -> 38.8 us (level)
  the two profiles are of different devices: /device:TPU:49 before, /device:TPU:9 now
where the time goes in v5:
time: 38.8 us; the launch traced here: 38.6 us
  Pallas kernels  35.6 us (92%)
  local copies, waits for them, and re-layouts  2.38 us (6%)
  between operations  0.66 us (2%)
    pallas_call x1, Pallas kernels, move(): pl.pallas_call(functools.partial(kernel, s), out_shape=jax.ShapeDtypeStru...  35.6 us
    slice x1, local copies, waits for them, and re-layouts, per_device(): offsets[2] > 0  1.24 us
    unnamed x1, local copies, waits for them, and re-layouts  1.15 us

profile of v5, /device:TPU:9, one launch (start us, length us, event | category | flops | bytes accessed | tf_op | source)
XLA Modules:
  0.0 38.6 jit_solution(7636158818274663546)
XLA Ops:
  0.0 1.2 %slice.3 = s32[1]{0:T(128)} slice(s32[4]{0:T(128)} %param.9), slice={[2:3]} | slice | bytes 8 | tf_op jit(solution)/shard_map/slice | solution.py:742
  1.9 35.6 %conditional.1 = (f32[3,64,16,128]{3,2,1,0:T(8,128)S(1)}) conditional(s32[]{:T(128)} %bitcast.6, (s32[4]{0:T(128)}, f32[64]{0:T(128)}, f32[3,64,16,128]{3,2,1,0:T(8,128)}, f32[3,6,34,64]{3,2,1,0:T(8,128)}) %tuple.18, (s32[4]{0:T(128)}, f32[64]{0:T(128)}, f32[3,64,16,128]{3,2,1,0:T(8,128)}, f32[3,6,34,64]{3,2,1,0:T(8,128)}) %tuple.19), branch_computations={%region_0.0_spmd, %region_1.0_spmd} | conditional | bytes 8 | solution.py:741
  1.9 35.6 %branch_0_fun.1 = f32[3072,128]{1,0:T(8,128)S(1)} custom-call(s32[4]{0:T(128)} %get-tuple-element.25.off_hbm, f32[64]{0:T(128)} %get-tuple-element.40.stiff_hbm, f32[3,1024,128]{2,1,0:T(8,128)} %bitcast.10, f32[18,34,64]{2,1,0:T(8,128)} %bitcast.14), custom_call_target="tpu_custom_call" | custom-call | tf_op jit(solution)/shard_map/cond/branch_0_fun/pallas_call | solution.py:726
  37.5 1.1 %copy.14 = f32[3,64,16,128]{3,2,1,0:T(8,128)} copy(f32[3,64,16,128]{3,2,1,0:T(8,128)S(1)} %get-tuple-element.33) | data formatting | bytes 3145728
